TPU v7x, 128 devices: a whole 4x4x4 slice. The times are simulated.
128 devices in a mesh: row: 8 (over y, x_lo), col: 16 (over x_hi, z, core).
Axes of the slice: x: 4 (x_hi: 2, x_lo: 2; x = x_hi * 2 + x_lo), y: 4, z: 4, core: 2. Of those that a mesh axis runs over, the one named last changes fastest.
Arguments:
- centres: float32 [40960, 64], P(('row', 'col')), may hold values from -6 to 6
- targets: float32 [40960, 16], P(('row', 'col')), may hold values from -6 to 6
- start_weights: float32 [40960, 16], P(('row', 'col')), may hold values from -6 to 6
Outputs:
- weighted: float32 [40960, 16], P(('row', 'col'))
- residual: float32 [40960, 16], P(('row', 'col'))
All inputs are finite; a program needn't handle non-finite values.
Results may differ from a plain program's by a relative error of at most 0.0003.
Values sent between devices are 32-bit elements; how exact they have to be, the bound alone decides.
No kernel may reach another device: no remote copies, remote signals or barrier semaphores. Data moves between devices by JAX's collectives and lax.ppermute only.
A program may use at most 128 MiB of HBM per device.

v0:
```python
import jax
import jax.numpy as jnp
from jax import lax
from jax.sharding import PartitionSpec as P

ITERS = 2


kernel_width = 2.0
soften = 0.01
ridge_term = 0.25


def kernel_block(left_pts, right_pts):
    left_sq = jnp.sum(left_pts * left_pts, axis=1)[:, None]
    right_sq = jnp.sum(right_pts * right_pts, axis=1)[None, :]
    cross = jnp.dot(
        left_pts, right_pts.T, precision=lax.Precision.HIGHEST, preferred_element_type=jnp.float32
    )
    return jnp.exp(-jnp.sqrt(left_sq + right_sq - 2.0 * cross + soften) / kernel_width)


def split_count(total):
    pieces = max(1, total // 512)
    while total % pieces:
        pieces -= 1
    return pieces


def stacked_rows(row_pts):
    pieces = split_count(row_pts.shape[0])
    return row_pts.reshape(pieces, row_pts.shape[0] // pieces, row_pts.shape[1])


def per_device(centres, targets, start_weights):
    row_pts = lax.all_gather(centres, "col", axis=0, tiled=True)
    col_pts = lax.all_gather(centres, "row", axis=0, tiled=True)
    nrows = row_pts.shape[0]
    ncols = col_pts.shape[0]
    stacked = stacked_rows(row_pts)
    tile = lax.map(lambda left_pts: kernel_block(left_pts, col_pts), stacked).reshape(nrows, ncols)
    partial_sums = jnp.sum(tile, axis=1)
    totals = lax.psum_scatter(partial_sums, "col", scatter_dimension=0, tiled=True)
    weighted = start_weights
    residual = targets
    for step in range(ITERS):
        scaled = weighted / totals[:, None]
        gathered = lax.all_gather(scaled, "row", axis=0, tiled=True)
        applied = lax.psum_scatter(
            jnp.dot(
                tile, gathered, precision=lax.Precision.HIGHEST, preferred_element_type=jnp.float32
            ),
            "col",
            scatter_dimension=0,
            tiled=True,
        )
        residual = targets - applied - ridge_term * weighted
        weighted = weighted + residual
    return (weighted, residual)


def solution(mesh):
    placed = (P(("row", "col"), None), P(("row", "col"), None), P(("row", "col"), None))
    return jax.shard_map(
        per_device,
        mesh=mesh,
        in_specs=placed,
        out_specs=(P(("row", "col"), None), P(("row", "col"), None)),
        check_vma=False,
    )
```

profile of v0, /device:TPU:0, one launch (start us, length us, event | category | flops | bytes accessed | tf_op | source)
XLA Modules:
  0.0 546.6 jit_solution(14569816624944917782)
XLA Ops:
  7.2 0.7 all-gather.6.cloned.1.call-update
  8.0 32.7 %all-gather.1 = f32[8,320,64]{1,2,0:T(8,128)S(1)} all-gather(f32[1,320,64]{1,2,0:T(8,128)} %bitcast.41), channel_id=1, replica_groups=mesh['row'=8,'col'=16] {'row'}, dimensions={0}, use_global_device_ids=true | all-gather | bytes 737280 | tf_op jit(solution)/shard_map/all_gather | solution.py:37
  40.7 0.5 copy.14
  41.1 0.2 reshape.19
  41.3 1.5 copy.16
  42.8 0.6 dynamic-slice
  44.1 15.9 %all-gather.6.cloned.1.call-done = f32[16,320,64]{1,2,0:T(8,128)} async-done(((f32[1,320,64]{1,2,0:T(8,128)}), f32[16,320,64]{1,2,0:T(8,128)}) %all-gather.6.cloned.1.call-update) | async-done | bytes 1310736 | tf_op jit(solution)/shard_map/all_gather | solution.py:36
  60.0 2.0 copy.19
  62.0 99.3 %while.12 = (s32[]{:T(128)}, f32[10,512,2560]{2,1,0:T(8,128)}, f32[10,512,64]{2,1,0:T(8,128)S(1)}, f32[2560]{0:T(1024)S(1)}, f32[2560,64]{1,0:T(8,128)}, /*index=5*/s32[]{:T(128)}) while((s32[]{:T(128)}, f32[10,512,2560]{2,1,0:T(8,128)}, f32[10,512,64]{2,1,0:T(8,128)S(1)}, f32[2560]{0:T(1024)S(1)}, f32[2560,64]{1,0:T(8,128)}, ...), condition=%wide.region_3.4_spmd, body=%wide.region_1.3_spmd.sunk | while | flops 1014562304 | bytes 6964297 | solution.py:41
  62.0 0.2 fusion.17
  62.1 9.8 %bitcast_dynamic-update-slice_fusion.2 = f32[10,512,2560]{2,1,0:T(8,128)} fusion(f32[10,512,2560]{2,1,0:T(8,128)} %get-tuple-element.115, s32[]{:T(128)} %get-tuple-element.114, f32[2560,64]{1,0:T(8,128)} %get-tuple-element.124, f32[2560]{0:T(1024)S(1)} %get-tuple-element.123, f32[512]{0:T(512)S(1)} %fusion.17, f32[10,512,64]{2,1,0:T(8,128)S(1)} %get-tuple-element.122), kind=kOutput, calls=%fused_computation.clone.1 | convolution fusion | flops 1014497280 | bytes 6831104 | tf_op jit(solution)/shard_map/while/body/eval_jaxpr/dot_general | solution.py:17
  72.0 0.1 fusion.17
  72.1 9.8 %bitcast_dynamic-update-slice_fusion.2 = f32[10,512,2560]{2,1,0:T(8,128)} fusion(f32[10,512,2560]{2,1,0:T(8,128)} %get-tuple-element.115, s32[]{:T(128)} %get-tuple-element.114, f32[2560,64]{1,0:T(8,128)} %get-tuple-element.124, f32[2560]{0:T(1024)S(1)} %get-tuple-element.123, f32[512]{0:T(512)S(1)} %fusion.17, f32[10,512,64]{2,1,0:T(8,128)S(1)} %get-tuple-element.122), kind=kOutput, calls=%fused_computation.clone.1 | convolution fusion | flops 1014497280 | bytes 6831104 | tf_op jit(solution)/shard_map/while/body/eval_jaxpr/dot_general | solution.py:17
  82.1 9.7 %bitcast_dynamic-update-slice_fusion.2 = f32[10,512,2560]{2,1,0:T(8,128)} fusion(f32[10,512,2560]{2,1,0:T(8,128)} %get-tuple-element.115, s32[]{:T(128)} %get-tuple-element.114, f32[2560,64]{1,0:T(8,128)} %get-tuple-element.124, f32[2560]{0:T(1024)S(1)} %get-tuple-element.123, f32[512]{0:T(512)S(1)} %fusion.17, f32[10,512,64]{2,1,0:T(8,128)S(1)} %get-tuple-element.122), kind=kOutput, calls=%fused_computation.clone.1 | convolution fusion | flops 1014497280 | bytes 6831104 | tf_op jit(solution)/shard_map/while/body/eval_jaxpr/dot_general | solution.py:17
  92.0 9.7 %bitcast_dynamic-update-slice_fusion.2 = f32[10,512,2560]{2,1,0:T(8,128)} fusion(f32[10,512,2560]{2,1,0:T(8,128)} %get-tuple-element.115, s32[]{:T(128)} %get-tuple-element.114, f32[2560,64]{1,0:T(8,128)} %get-tuple-element.124, f32[2560]{0:T(1024)S(1)} %get-tuple-element.123, f32[512]{0:T(512)S(1)} %fusion.17, f32[10,512,64]{2,1,0:T(8,128)S(1)} %get-tuple-element.122), kind=kOutput, calls=%fused_computation.clone.1 | convolution fusion | flops 1014497280 | bytes 6831104 | tf_op jit(solution)/shard_map/while/body/eval_jaxpr/dot_general | solution.py:17
  101.9 9.8 %bitcast_dynamic-update-slice_fusion.2 = f32[10,512,2560]{2,1,0:T(8,128)} fusion(f32[10,512,2560]{2,1,0:T(8,128)} %get-tuple-element.115, s32[]{:T(128)} %get-tuple-element.114, f32[2560,64]{1,0:T(8,128)} %get-tuple-element.124, f32[2560]{0:T(1024)S(1)} %get-tuple-element.123, f32[512]{0:T(512)S(1)} %fusion.17, f32[10,512,64]{2,1,0:T(8,128)S(1)} %get-tuple-element.122), kind=kOutput, calls=%fused_computation.clone.1 | convolution fusion | flops 1014497280 | bytes 6831104 | tf_op jit(solution)/shard_map/while/body/eval_jaxpr/dot_general | solution.py:17
  111.8 9.8 %bitcast_dynamic-update-slice_fusion.2 = f32[10,512,2560]{2,1,0:T(8,128)} fusion(f32[10,512,2560]{2,1,0:T(8,128)} %get-tuple-element.115, s32[]{:T(128)} %get-tuple-element.114, f32[2560,64]{1,0:T(8,128)} %get-tuple-element.124, f32[2560]{0:T(1024)S(1)} %get-tuple-element.123, f32[512]{0:T(512)S(1)} %fusion.17, f32[10,512,64]{2,1,0:T(8,128)S(1)} %get-tuple-element.122), kind=kOutput, calls=%fused_computation.clone.1 | convolution fusion | flops 1014497280 | bytes 6831104 | tf_op jit(solution)/shard_map/while/body/eval_jaxpr/dot_general | solution.py:17
  121.8 9.7 %bitcast_dynamic-update-slice_fusion.2 = f32[10,512,2560]{2,1,0:T(8,128)} fusion(f32[10,512,2560]{2,1,0:T(8,128)} %get-tuple-element.115, s32[]{:T(128)} %get-tuple-element.114, f32[2560,64]{1,0:T(8,128)} %get-tuple-element.124, f32[2560]{0:T(1024)S(1)} %get-tuple-element.123, f32[512]{0:T(512)S(1)} %fusion.17, f32[10,512,64]{2,1,0:T(8,128)S(1)} %get-tuple-element.122), kind=kOutput, calls=%fused_computation.clone.1 | convolution fusion | flops 1014497280 | bytes 6831104 | tf_op jit(solution)/shard_map/while/body/eval_jaxpr/dot_general | solution.py:17
  131.7 9.7 %bitcast_dynamic-update-slice_fusion.2 = f32[10,512,2560]{2,1,0:T(8,128)} fusion(f32[10,512,2560]{2,1,0:T(8,128)} %get-tuple-element.115, s32[]{:T(128)} %get-tuple-element.114, f32[2560,64]{1,0:T(8,128)} %get-tuple-element.124, f32[2560]{0:T(1024)S(1)} %get-tuple-element.123, f32[512]{0:T(512)S(1)} %fusion.17, f32[10,512,64]{2,1,0:T(8,128)S(1)} %get-tuple-element.122), kind=kOutput, calls=%fused_computation.clone.1 | convolution fusion | flops 1014497280 | bytes 6831104 | tf_op jit(solution)/shard_map/while/body/eval_jaxpr/dot_general | solution.py:17
  141.6 9.8 %bitcast_dynamic-update-slice_fusion.2 = f32[10,512,2560]{2,1,0:T(8,128)} fusion(f32[10,512,2560]{2,1,0:T(8,128)} %get-tuple-element.115, s32[]{:T(128)} %get-tuple-element.114, f32[2560,64]{1,0:T(8,128)} %get-tuple-element.124, f32[2560]{0:T(1024)S(1)} %get-tuple-element.123, f32[512]{0:T(512)S(1)} %fusion.17, f32[10,512,64]{2,1,0:T(8,128)S(1)} %get-tuple-element.122), kind=kOutput, calls=%fused_computation.clone.1 | convolution fusion | flops 1014497280 | bytes 6831104 | tf_op jit(solution)/shard_map/while/body/eval_jaxpr/dot_general | solution.py:17
  151.6 9.7 %bitcast_dynamic-update-slice_fusion.2 = f32[10,512,2560]{2,1,0:T(8,128)} fusion(f32[10,512,2560]{2,1,0:T(8,128)} %get-tuple-element.115, s32[]{:T(128)} %get-tuple-element.114, f32[2560,64]{1,0:T(8,128)} %get-tuple-element.124, f32[2560]{0:T(1024)S(1)} %get-tuple-element.123, f32[512]{0:T(512)S(1)} %fusion.17, f32[10,512,64]{2,1,0:T(8,128)S(1)} %get-tuple-element.122), kind=kOutput, calls=%fused_computation.clone.1 | convolution fusion | flops 1014497280 | bytes 6831104 | tf_op jit(solution)/shard_map/while/body/eval_jaxpr/dot_general | solution.py:17
  161.3 16.9 %reduce_sum.34 = f32[10,512]{1,0:T(8,128)S(1)} reduce(f32[10,512,2560]{2,1,0:T(8,128)} %get-tuple-element.57, f32[]{:T(128)} %constant.38.clone.1), dimensions={2}, to_apply=%region_4.5 | reduce | flops 13102080 | bytes 52449284 | tf_op jit(solution)/shard_map/reduce_sum | solution.py:42
  178.2 67.1 %all-reduce = f32[5120]{0:T(1024)S(1)} all-reduce(f32[5120]{0:T(1024)S(1)} %reduce_sum.35), channel_id=2, replica_groups=mesh['row'=8,'col'=16] {'col'}, use_global_device_ids=true, to_apply=%region_5.6.clone | all-reduce | flops 5120 | bytes 40960
  245.4 28.8 %all-gather.2 = f32[8,320,16]{1,2,0:T(8,128)S(1)} all-gather(f32[1,320,16]{1,2,0:T(8,128)S(1)} %divide_bitcast_fusion.1), channel_id=1, replica_groups=mesh['row'=8,'col'=16] {'row'}, dimensions={0}, use_global_device_ids=true | all-gather | bytes 184320 | tf_op jit(solution)/shard_map/all_gather | solution.py:48
  274.4 45.3 %fusion.5 = f32[5120,16]{1,0:T(8,128)} fusion(f32[5120,2560]{1,0:T(8,128)} %bitcast.37, f32[2560,16]{0,1:T(8,128)S(1)} %reshape.21), kind=kOutput, calls=%fused_computation.12 | convolution fusion | flops 2516582400 | bytes 52920320
  319.7 71.7 %reduce-scatter.7.cloned.1.call-done = f32[320,16]{1,0:T(8,128)} async-done(((f32[5120,16]{1,0:T(8,128)}), f32[320,16]{1,0:T(8,128)}) %reduce-scatter.7.cloned.1.call-update) | async-done | bytes 20496
  391.4 1.0 copy.21
  392.5 28.8 %all-gather.3 = f32[8,320,16]{1,2,0:T(8,128)S(1)} all-gather(f32[1,320,16]{1,2,0:T(8,128)S(1)} %get-tuple-element.75), channel_id=1, replica_groups=mesh['row'=8,'col'=16] {'row'}, dimensions={0}, use_global_device_ids=true | all-gather | bytes 184320 | tf_op jit(solution)/shard_map/all_gather | solution.py:48
  421.4 45.3 %fusion.6 = f32[5120,16]{1,0:T(8,128)} fusion(f32[5120,2560]{1,0:T(8,128)} %bitcast.38, f32[2560,16]{0,1:T(8,128)S(1)} %reshape.23), kind=kOutput, calls=%fused_computation.13 | convolution fusion | flops 2516582400 | bytes 52920320
  466.8 71.7 %reduce-scatter.9.cloned.1.call-done = f32[320,16]{1,0:T(8,128)} async-done(((f32[5120,16]{1,0:T(8,128)}), f32[320,16]{1,0:T(8,128)}) %reduce-scatter.9.cloned.1.call-update) | async-done | bytes 20496
  538.4 1.0 copy.23
  539.4 0.6 fusion.4
  (29 shorter events, 1.9 us)
Async XLA Ops:
  7.2 35.6 %copy-start.2 = (u32[128]{0:T(128)S(1)}, u32[128]{0:T(128)}, u32[]{:S(2)}) copy-start(u32[128]{0:T(128)} %constant.45) | copy-start | bytes 1540
  7.2 52.8 %all-gather.6.cloned.1.call-start = ((), (), s32[]{:S(2)}) async-start(), calls=%async_computation.2 | async-start | bytes 1671168 | tf_op jit(solution)/shard_map/all_gather | solution.py:36
  7.9 383.5 %reduce-scatter.7.cloned.1.call-start = ((), (), s32[]{:S(2)}) async-start(), calls=%async_computation.3 | async-start | bytes 2785280
  161.3 84.1 %copy-start = (f32[320,16]{0,1:T(8,128)S(1)}, f32[320,16]{0,1:T(8,128)}, u32[]{:S(2)}) copy-start(f32[320,16]{0,1:T(8,128)} %param.7) | copy-start | bytes 61444
  274.3 118.1 %copy-start.1 = (f32[320,16]{0,1:T(8,128)S(1)}, f32[320,16]{0,1:T(8,128)}, u32[]{:S(2)}) copy-start(f32[320,16]{0,1:T(8,128)} %param.6) | copy-start | bytes 61444
  319.7 218.8 %reduce-scatter.9.cloned.1.call-start = ((), (), s32[]{:S(2)}) async-start(), calls=%async_computation.4 | async-start | bytes 2785280
Sparse Core Ops, SparseCore 0:
  10.5 49.4 all-gather.5
  319.8 71.6 reduce-scatter.6
  466.9 71.5 reduce-scatter.8
where the time goes:
time: 547 us
  matrix products  188 us (34%)
  waiting for transfers between devices  160 us (29%)
  blocking collectives  157 us (29%)
  other arithmetic  19.1 us (3%)
  between operations  14.5 us (3%)
  local copies, waits for them, and re-layouts  7.08 us (1%)
    unnamed x5, waiting for transfers between devices  144 us
    dot_general x10, matrix products, kernel_block(): jnp.dot(left_pts, right_pts.T, precision=lax.Precision.HIGHEST, preferred...  97.8 us
    unnamed x2, matrix products  90.6 us
    unnamed x1, blocking collectives  67.1 us
    all_gather x2, blocking collectives, per_device(): gathered = lax.all_gather(scaled, 'row', axis=0, tiled=True)  57.6 us
    all_gather x1, blocking collectives, per_device(): col_pts = lax.all_gather(centres, 'row', axis=0, tiled=True)  32.7 us
    reduce_sum x1, other arithmetic, per_device(): partial_sums = jnp.sum(tile, axis=1)  16.9 us
    all_gather x1, waiting for transfers between devices, per_device(): row_pts = lax.all_gather(centres, 'col', axis=0, tiled=True)  15.9 us
  transfers between devices with their start and end apart: 3, of which 3 were waited for; matrix products, arithmetic and copies ran while one was open for 1% of the time, Pallas kernels for 0%

commit v1 on v0

v1 whole, which is shorter than its diff:
```python
import jax
import jax.numpy as jnp
from jax import lax
from jax.experimental import pallas as pl
from jax.experimental.pallas import tpu as pltpu
from jax.sharding import Mesh, PartitionSpec as P

ITERS = 2

kernel_width = 2.0
soften = 0.01
ridge_term = 0.25

SCALE = 1.4426950408889634 / kernel_width
FLOOR = soften * SCALE * SCALE

f32 = jnp.float32
bf16 = jnp.bfloat16

AXES = ("y", "xl", "xh", "z", "k")
BLK = 320
FEAT = 64
TGT = 16
QUART = 4 * BLK
COLS = 8 * BLK
HALF = COLS // 2
IN_VMEM = 2

WHOLE = pl.BlockSpec(memory_space=pltpu.VMEM)
ANY = pl.BlockSpec(memory_space=pl.ANY)


def params(mib):
    return pltpu.CompilerParams(vmem_limit_bytes=mib << 20)


def parts_of(pts):
    scaled = pts * SCALE
    high = scaled.astype(bf16)
    low = (scaled - high.astype(f32)).astype(bf16)
    kept = high.astype(f32) + low.astype(f32)
    return high, low, jnp.sum(kept * kept, axis=0, keepdims=True)


def gram_setup(rows_ref, cols_ref, lhs, rhs, row_sq, col_sq):
    high, low, sq = parts_of(cols_ref[0:FEAT, :])
    rhs[0:64, :] = high
    rhs[64:128, :] = low
    rhs[128:192, :] = high
    rhs[192:256, :] = low
    col_sq[...] = sq
    pts = rows_ref[0:FEAT, :].T * SCALE
    high = pts.astype(bf16)
    low = (pts - high.astype(f32)).astype(bf16)
    kept = high.astype(f32) + low.astype(f32)
    row_sq[...] = jnp.sum(kept * kept, axis=1, keepdims=True) + FLOOR
    lhs[...] = jnp.concatenate([high, high, low, low], axis=1) * jnp.asarray(2.0, bf16)


def gram_cols(lhs, rhs_part, row_sq, col_part):
    cross = jnp.dot(lhs[...], rhs_part, preferred_element_type=f32)
    dist = jnp.maximum((row_sq[...] - cross) + col_part, FLOOR)
    return jnp.exp2(-(dist * lax.rsqrt(dist)))


def fold_lanes(part):
    acc = part[:, 0:128]
    for at in range(128, part.shape[1], 128):
        acc = acc + part[:, at : at + 128]
    return acc


def put_totals(acc, tot_ref):
    line = jnp.sum(acc.T, axis=0, keepdims=True)
    for m in range(4):
        tot_ref[m : m + 1, :] = line[:, m * BLK : (m + 1) * BLK]


def gram_quarter(rows, cols, keep):
    scratch = [
        pltpu.VMEM((QUART, 256), bf16),
        pltpu.VMEM((256, COLS), bf16),
        pltpu.VMEM((QUART, 1), f32),
        pltpu.VMEM((1, COLS), f32),
        pltpu.VMEM((QUART, 128), f32),
    ]
    step_cols = 256 if keep else 512

    def kept_body(rows_ref, cols_ref, out_ref, tot_ref, lhs, rhs, row_sq, col_sq, acc):
        gram_setup(rows_ref, cols_ref, lhs, rhs, row_sq, col_sq)
        for at in range(0, COLS, step_cols):
            part = gram_cols(lhs, rhs[:, at : at + step_cols], row_sq, col_sq[:, at : at + step_cols])
            out_ref[:, at : at + step_cols] = part
            if at:
                acc[...] += fold_lanes(part)
            else:
                acc[...] = fold_lanes(part)
        put_totals(acc[...], tot_ref)

    def sent_body(rows_ref, cols_ref, out_ref, tot_ref, lhs, rhs, row_sq, col_sq, acc):
        step = pl.program_id(0)

        @pl.when(step == 0)
        def _():
            gram_setup(rows_ref, cols_ref, lhs, rhs, row_sq, col_sq)
            acc[...] = jnp.zeros_like(acc)

        here = pl.ds(pl.multiple_of(step * step_cols, step_cols), step_cols)
        part = gram_cols(lhs, rhs[:, here], row_sq, col_sq[:, here])
        out_ref[...] = part
        acc[...] += fold_lanes(part)

        @pl.when(step == pl.num_programs(0) - 1)
        def _():
            put_totals(acc[...], tot_ref)

    tot = jax.ShapeDtypeStruct((4, BLK), f32)
    if keep:
        return pl.pallas_call(
            kept_body,
            in_specs=[WHOLE, WHOLE],
            out_specs=[WHOLE, WHOLE],
            out_shape=[pltpu.VMEM((QUART, COLS), f32), tot],
            scratch_shapes=scratch,
            compiler_params=params(20),
            name="gram_kept",
        )(rows, cols)
    return pl.pallas_call(
        sent_body,
        grid=(COLS // step_cols,),
        in_specs=[pl.BlockSpec(rows.shape, lambda j: (0, 0)), pl.BlockSpec(cols.shape, lambda j: (0, 0))],
        out_specs=[pl.BlockSpec((QUART, step_cols), lambda j: (0, j)), pl.BlockSpec((4, BLK), lambda j: (0, 0))],
        out_shape=[jax.ShapeDtypeStruct((QUART, COLS), f32), tot],
        scratch_shapes=scratch,
        compiler_params=params(24),
        name="gram_sent",
    )(rows, cols)


def two_terms(vals):
    high = vals.astype(bf16)
    return high, (vals - high.astype(f32)).astype(bf16)


PIECE = 640


def chunk_plan():
    kept = [(q, at) for q in range(IN_VMEM) for at in range(0, QUART, PIECE)]
    fetched = [(q, at) for q in range(IN_VMEM, 4) for at in range(0, QUART, PIECE)]
    order = []
    for n in range(max(len(kept), len(fetched))):
        order += kept[n : n + 1] + fetched[n : n + 1]
    return order, fetched


def apply_down(scaled, tiles, first):
    order, fetched = chunk_plan()
    slots = 3

    def body(*refs):
        s_ref, tile_refs, out_ref, held, sems = refs[0], refs[1:5], refs[5], refs[6], refs[7]

        def fetch(n):
            q, at = fetched[n]
            return pltpu.make_async_copy(
                tile_refs[q].at[pl.ds(at, PIECE), pl.ds(first, HALF)], held.at[n % slots], sems.at[n % slots]
            )

        for n in range(min(slots, len(fetched))):
            fetch(n).start()
        acc = None
        for q, at in order:
            if q < IN_VMEM:
                piece = tile_refs[q][at : at + PIECE, first : first + HALF]
            else:
                n = fetched.index((q, at))
                fetch(n).wait()
                piece = held[n % slots]
            s_hi, s_lo = two_terms(s_ref[:, q * QUART + at : q * QUART + at + PIECE])
            both = jnp.concatenate([s_hi, s_lo], axis=0)
            hi, lo = two_terms(piece)
            part = jnp.dot(both, hi, preferred_element_type=f32) + jnp.dot(both, lo, preferred_element_type=f32)
            if acc is None:
                out_ref[...] = part[0:16] + part[16:32]
                acc = True
            else:
                out_ref[...] += part[0:16] + part[16:32]
            if q >= IN_VMEM and n + slots < len(fetched):
                fetch(n + slots).start()

    return pl.pallas_call(
        body,
        in_specs=[WHOLE] + [WHOLE if q < IN_VMEM else ANY for q in range(4)],
        out_specs=WHOLE,
        out_shape=jax.ShapeDtypeStruct((TGT, HALF), f32),
        scratch_shapes=[pltpu.VMEM((slots, PIECE, HALF), f32), pltpu.SemaphoreType.DMA((slots,))],
        compiler_params=params(24),
        name="apply_down",
    )(scaled, *tiles)


def apply_across(scaled, tile, keep):
    step_rows = 640 if keep else 320

    def column_form(s_ref, held):
        s_hi, s_lo = two_terms(s_ref[...])
        held[...] = jnp.concatenate([s_hi.astype(f32), s_lo.astype(f32)], axis=0).T.astype(bf16)

    def product(piece, held):
        hi, lo = two_terms(piece)
        out = jnp.dot(hi, held[...], preferred_element_type=f32) + jnp.dot(lo, held[...], preferred_element_type=f32)
        out = out.T
        return out[0:16] + out[16:32]

    def kept_body(s_ref, tile_ref, out_ref, held):
        column_form(s_ref, held)
        for at in range(0, QUART, step_rows):
            out_ref[:, at : at + step_rows] = product(tile_ref[at : at + step_rows, :], held)

    def sent_body(s_ref, tile_ref, out_ref, held, ring, sems):
        def fetch(n):
            return pltpu.make_async_copy(
                tile_ref.at[pl.ds(n * step_rows, step_rows), :], ring.at[n % 3], sems.at[n % 3]
            )

        count = QUART // step_rows
        for n in range(3):
            fetch(n).start()
        column_form(s_ref, held)
        lines = []
        for n in range(count):
            fetch(n).wait()
            lines.append(product(ring[n % 3], held))
            if n + 3 < count:
                fetch(n + 3).start()
        out_ref[...] = jnp.concatenate(lines, axis=1)

    held = pltpu.VMEM((COLS, 32), bf16)
    return pl.pallas_call(
        kept_body if keep else sent_body,
        in_specs=[WHOLE, WHOLE if keep else ANY],
        out_specs=WHOLE,
        out_shape=jax.ShapeDtypeStruct((TGT, QUART), f32),
        scratch_shapes=[held]
        + ([] if keep else [pltpu.VMEM((3, step_rows, COLS), f32), pltpu.SemaphoreType.DMA((3,))]),
        compiler_params=params(24),
        name="apply_across",
    )(scaled, tile)


def swap(x, axis, by):
    n = 2 if axis == "k" else 4
    return lax.ppermute(x, axis, [(i, i ^ by) for i in range(n)])


X = ("xl", "xh")


def per_device(centres, targets, start_weights):
    pts, goal, start = centres.T, targets.T, start_weights.T
    ahead = goal + (1.0 - ridge_term) * start
    row_block = jnp.concatenate([pts, start], axis=0)
    col_block = jnp.concatenate([pts, ahead], axis=0)
    by_z = [row_block] + [swap(row_block, "z", m) for m in (1, 2, 3)]
    by_y = [col_block] + [swap(col_block, "y", m) for m in (1, 2, 3)]
    col_own = jnp.concatenate(by_y, axis=1)
    row_own = jnp.concatenate(by_z, axis=1)
    cols = jnp.concatenate([col_own[:FEAT], swap(col_own[:FEAT], "k", 1)], axis=1)
    rows = [row_own] + [swap(row_own, X, m) for m in (1, 2, 3)]

    tiles, tots = [], []
    for q in range(4):
        tile, tot = gram_quarter(rows[q], cols, q < IN_VMEM)
        tiles.append(tile)
        tots.append(tot)
    totals = jnp.stack(tots)
    from_z = [totals] + [swap(totals, "z", m) for m in (1, 2, 3)]
    totals = sum(
        jnp.stack([from_z[j][:, m ^ j] for m in range(4)], axis=1) for j in range(4)
    )
    from_x = [totals] + [swap(totals, X, m) for m in (1, 2, 3)]
    totals = sum(jnp.stack([from_x[j][m ^ j] for m in range(4)]) for j in range(4))
    own_tot = totals[0, 0][None, :]

    all_rows = jnp.concatenate([r[FEAT:] for r in rows], axis=1)
    scaled = all_rows / totals.reshape(1, 4 * QUART)

    other = apply_down(scaled, tiles, HALF)
    sent = swap(other, "k", 1)
    own = apply_down(scaled, tiles, 0) + sent
    packed = jnp.concatenate([own, jnp.pad(own_tot, ((0, 7), (0, QUART - BLK)))], axis=0)
    from_y = [packed] + [swap(packed, "y", m) for m in (1, 2, 3)]
    applied = 0.0
    for j in range(4):
        got = from_y[j][:TGT]
        applied = applied + jnp.concatenate(
            [got[:, (m ^ j) * BLK : ((m ^ j) + 1) * BLK] for m in range(4)], axis=1
        )
    col_tot = jnp.concatenate([from_y[j][TGT : TGT + 1, :BLK] for j in range(4)], axis=1)
    weighted = col_own[FEAT:] - applied
    scaled = weighted / col_tot
    scaled = jnp.concatenate([scaled, swap(scaled, "k", 1)], axis=1)

    moved = None
    total = None
    parts = {}
    for q in (1, 2, 3, 0):
        parts[q] = apply_across(scaled, tiles[q], q < IN_VMEM)
        if q:
            parts[q] = swap(parts[q], X, q)
    total = parts[0] + parts[1] + parts[2] + parts[3]
    applied = total[:, :BLK]
    for m in (1, 2, 3):
        applied = applied + swap(total[:, m * BLK : (m + 1) * BLK], "z", m)
    weighted = weighted[:, :BLK]
    residual = goal - applied - ridge_term * weighted
    weighted = weighted + residual
    return weighted.T, residual.T


def solution(mesh):
    fine = Mesh(mesh.devices.reshape(4, 2, 2, 4, 2), AXES)
    placed = P(AXES, None)
    return jax.shard_map(
        per_device, mesh=fine, in_specs=(placed,) * 3, out_specs=(placed,) * 2, check_vma=False
    )
```

time: 547 us -> 182 us (0.33)
  matrix products: 188 us -> 0 us
  blocking collectives: 157 us -> 0 us
  waiting for transfers between devices: 160 us -> 32.7 us
  Pallas kernels: 0 us -> 64 us
  local copies, waits for them, and re-layouts: 7.08 us -> 43.6 us
  starting transfers between devices: 0.12 us -> 34.6 us
  other arithmetic: 19.1 us -> 2.6 us
  between operations: 14.5 us -> 1.2 us
    unnamed x5 -> x0, waiting for transfers between devices: 144 us -> none
    dot_general x10 -> x0, matrix products: 97.8 us -> none  [kernel_block(): jnp.dot(left_pts, right_pts.T, precision=lax.Precision.HIGHEST, preferred...]
    unnamed x2 -> x0, matrix products: 90.6 us -> none
    all_gather x3 -> x0, blocking collectives: 90.3 us -> none  [the longest x2 57.6 us: per_device(): gathered = lax.all_gather(scaled, 'row', axis=0, tiled=True)]
    unnamed x1 -> x0, blocking collectives: 67.1 us -> none
    pallas_call x0 -> x10, Pallas kernels: none -> 64 us  [the longest x4 26.7 us: apply_across(): pl.pallas_call(kept_body if keep else sent_body, in_specs=[WHOLE, WHOLE i...]
    unnamed x12 -> x28, local copies, waits for them, and re-layouts: 2.85 us -> 42.6 us
    ppermute x0 -> x27, starting transfers between devices: none -> 34.6 us  [swap(): return lax.ppermute(x, axis, [(i, i ^ by) for i in range(n)])]
  transfers between devices with their start and end apart: 3 -> 27, of which waited for: 3 -> 14; matrix products, arithmetic and copies ran while one was open for 1% -> 0% of each run, Pallas kernels for 0% -> 16%
where the time goes in v1:
time: 182 us; the launch traced here: 179 us
  Pallas kernels  64 us (35%)
  local copies, waits for them, and re-layouts  43.6 us (24%)
  starting transfers between devices  34.6 us (19%)
  waiting for transfers between devices  32.7 us (18%)
  other arithmetic  2.6 us (1%)
    unnamed x28, local copies, waits for them, and re-layouts  42.6 us
    ppermute x27, starting transfers between devices, swap(): return lax.ppermute(x, axis, [(i, i ^ by) for i in range(n)])  34.6 us
    ppermute x27, waiting for transfers between devices, swap(): return lax.ppermute(x, axis, [(i, i ^ by) for i in range(n)])  32.7 us
    pallas_call x4, Pallas kernels, apply_across(): pl.pallas_call(kept_body if keep else sent_body, in_specs=[WHOLE, WHOLE i...  26.7 us
    pallas_call x2, Pallas kernels, gram_quarter(): pl.pallas_call(sent_body, grid=(COLS // step_cols,), in_specs=[pl.BlockSp...  14.7 us
    pallas_call x2, Pallas kernels, apply_down(): pl.pallas_call(body, in_specs=[WHOLE] + [WHOLE if q < IN_VMEM else ANY fo...  11.8 us
    pallas_call x2, Pallas kernels, gram_quarter(): pl.pallas_call(kept_body, in_specs=[WHOLE, WHOLE], out_specs=[WHOLE, WHOL...  10.8 us
  transfers between devices with their start and end apart: 27, of which 14 were waited for; matrix products, arithmetic and copies ran while one was open for 0% of the time, Pallas kernels for 16%

profile of v1, /device:TPU:0, one launch (start us, length us, event | category | flops | bytes accessed | tf_op | source)
XLA Modules:
  0.0 178.7 jit_solution(9499089428961460328)
XLA Ops:
  2.3 3.2 %collective-permute-start.2 = (f32[80,320]{1,0:T(8,128)S(1)}, f32[80,320]{1,0:T(8,128)S(1)}, u32[]{:S(2)}, u32[]{:S(2)}) collective-permute-start(f32[80,320]{1,0:T(8,128)S(1)} %get-tuple-element.32), channel_id=1, source_target_pairs={{0,96},{32,64},{64,32},{96,0},{1,97},{33,65},{65,33},{97,1},{2,98}... | collective-permute-start | bytes 307208 | tf_op jit(solution)/shard_map/ppermute | solution.py:254
  6.5 4.2 %collective-permute-done.2 = f32[80,320]{1,0:T(8,128)S(1)} collective-permute-done((f32[80,320]{1,0:T(8,128)S(1)}, f32[80,320]{1,0:T(8,128)S(1)}, u32[]{:S(2)}, u32[]{:S(2)}) %collective-permute-start.2) | collective-permute-done | bytes 102432 | tf_op jit(solution)/shard_map/ppermute | solution.py:254
  10.7 2.4 %collective-permute-done.1 = f32[80,320]{1,0:T(8,128)S(1)} collective-permute-done((f32[80,320]{1,0:T(8,128)S(1)}, f32[80,320]{1,0:T(8,128)S(1)}, u32[]{:S(2)}, u32[]{:S(2)}) %collective-permute-start.1) | collective-permute-done | bytes 102432 | tf_op jit(solution)/shard_map/ppermute | solution.py:254
  13.4 4.1 %collective-permute-start.5 = (f32[80,320]{1,0:T(8,128)S(1)}, f32[80,320]{1,0:T(8,128)S(1)}, u32[]{:S(2)}, u32[]{:S(2)}) collective-permute-start(f32[80,320]{1,0:T(8,128)S(1)} %get-tuple-element.33), channel_id=1, source_target_pairs={{0,6},{2,4},{4,2},{6,0},{1,7},{3,5},{5,3},{7,1},{8,14},{10,12},{12... | collective-permute-start | bytes 307208 | tf_op jit(solution)/shard_map/ppermute | solution.py:254
  18.4 4.9 %collective-permute-done.5 = f32[80,320]{1,0:T(8,128)S(1)} collective-permute-done((f32[80,320]{1,0:T(8,128)S(1)}, f32[80,320]{1,0:T(8,128)S(1)}, u32[]{:S(2)}, u32[]{:S(2)}) %collective-permute-start.5) | collective-permute-done | bytes 102432 | tf_op jit(solution)/shard_map/ppermute | solution.py:254
  25.3 3.1 %collective-permute-start.6 = (f32[80,1280]{1,0:T(8,128)S(1)}, f32[80,1280]{1,0:T(8,128)S(1)}, u32[]{:S(2)}, u32[]{:S(2)}) collective-permute-start(f32[80,1280]{1,0:T(8,128)S(1)} %concatenate.42.rows_ref), channel_id=1, source_target_pairs={{0,8},{8,0},{16,24},{24,16},{1,9},{9,1},{17,25},{25,17},{2,10},{10... | collective-permute-start | bytes 1228808 | tf_op jit(solution)/shard_map/ppermute | solution.py:254
  29.9 5.4 %gram_kept.2 = (f32[1280,2560]{1,0:T(8,128)S(1)}, f32[4,320]{1,0:T(4,128)S(1)}) custom-call(f32[80,1280]{1,0:T(8,128)S(1)} %concatenate.42.rows_ref, f32[64,2560]{1,0:T(8,128)S(1)} %pad_maximum_fusion.cols_ref), custom_call_target="tpu_custom_call" | custom-call | tf_op jit(solution)/shard_map/gram_kept/pallas_call | solution.py:119
  35.3 4.8 %copy-done = f32[1280,2560]{1,0:T(8,128)} copy-done((f32[1280,2560]{1,0:T(8,128)}, f32[1280,2560]{1,0:T(8,128)S(1)}, u32[]{:S(2)}) %copy-start) | copy-done | bytes 13107224
  40.1 5.4 %gram_kept.3 = (f32[1280,2560]{1,0:T(8,128)S(1)}, f32[4,320]{1,0:T(4,128)S(1)}) custom-call(f32[80,1280]{1,0:T(8,128)S(1)} %collective-permute-done.6.rows_ref, f32[64,2560]{1,0:T(8,128)S(1)} %pad_maximum_fusion.cols_ref), custom_call_target="tpu_custom_call" | custom-call | tf_op jit(solution)/shard_map/gram_kept/pallas_call | solution.py:119
  45.5 4.8 %copy-done.2 = f32[1280,2560]{1,0:T(8,128)} copy-done((f32[1280,2560]{1,0:T(8,128)}, f32[1280,2560]{1,0:T(8,128)S(1)}, u32[]{:S(2)}) %copy-start.2) | copy-done | bytes 13107224
  50.2 7.6 %gram_sent.2 = (f32[1280,2560]{1,0:T(8,128)S(1)}, f32[4,320]{1,0:T(4,128)S(1)}) custom-call(f32[80,1280]{1,0:T(8,128)S(1)} %collective-permute-done.7.rows_ref, f32[64,2560]{1,0:T(8,128)S(1)} %pad_maximum_fusion.cols_ref), custom_call_target="tpu_custom_call" | custom-call | tf_op jit(solution)/shard_map/gram_sent/pallas_call | solution.py:128
  57.9 4.7 %copy-done.5 = f32[1280,2560]{1,0:T(8,128)} copy-done((f32[1280,2560]{1,0:T(8,128)}, f32[1280,2560]{1,0:T(8,128)S(1)}, u32[]{:S(2)}) %copy-start.5) | copy-done | bytes 13107224
  62.5 7.1 %gram_sent.3 = (f32[1280,2560]{1,0:T(8,128)S(1)}, f32[4,320]{1,0:T(4,128)S(1)}) custom-call(f32[80,1280]{1,0:T(8,128)S(1)} %collective-permute-done.8.rows_ref, f32[64,2560]{1,0:T(8,128)S(1)} %pad_maximum_fusion.cols_ref), custom_call_target="tpu_custom_call" | custom-call | tf_op jit(solution)/shard_map/gram_sent/pallas_call | solution.py:128
  69.6 4.8 %copy-done.7 = f32[1280,2560]{1,0:T(8,128)} copy-done((f32[1280,2560]{1,0:T(8,128)}, f32[1280,2560]{1,0:T(8,128)S(1)}, u32[]{:S(2)}) %copy-start.7) | copy-done | bytes 13107224
  74.4 2.3 %collective-permute-start.11 = (f32[4,4,320]{2,1,0:T(4,128)S(1)}, f32[4,4,320]{2,1,0:T(4,128)S(1)}, u32[]{:S(2)}, u32[]{:S(2)}) collective-permute-start(f32[4,4,320]{2,1,0:T(4,128)S(1)} %pad_maximum_fusion.4), channel_id=1, source_target_pairs={{0,4},{2,6},{4,0},{6,2},{1,5},{3,7},{5,1},{7,3},{8,12},{10,14},{12... | collective-permute-start | bytes 61448 | tf_op jit(solution)/shard_map/ppermute | solution.py:254
  83.5 2.2 %collective-permute-start.15 = (f32[4,4,320]{2,1,0:T(4,128)S(1)}, f32[4,4,320]{2,1,0:T(4,128)S(1)}, u32[]{:S(2)}, u32[]{:S(2)}) collective-permute-start(f32[4,4,320]{2,1,0:T(4,128)S(1)} %fusion.6), channel_id=1, source_target_pairs={{0,24},{8,16},{16,8},{24,0},{1,25},{9,17},{17,9},{25,1},{2,26},{10... | collective-permute-start | bytes 61448 | tf_op jit(solution)/shard_map/ppermute | solution.py:254
  86.4 2.2 %collective-permute-done.15 = f32[4,4,320]{2,1,0:T(4,128)S(1)} collective-permute-done((f32[4,4,320]{2,1,0:T(4,128)S(1)}, f32[4,4,320]{2,1,0:T(4,128)S(1)}, u32[]{:S(2)}, u32[]{:S(2)}) %collective-permute-start.15) | collective-permute-done | bytes 20512 | tf_op jit(solution)/shard_map/ppermute | solution.py:254
  88.6 2.4 %collective-permute-done.13 = f32[4,4,320]{2,1,0:T(4,128)S(1)} collective-permute-done((f32[4,4,320]{2,1,0:T(4,128)S(1)}, f32[4,4,320]{2,1,0:T(4,128)S(1)}, u32[]{:S(2)}, u32[]{:S(2)}) %collective-permute-start.13) | collective-permute-done | bytes 20512 | tf_op jit(solution)/shard_map/ppermute | solution.py:254
  91.1 4.7 %copy-done.1 = f32[1280,2560]{1,0:T(8,128)S(1)} copy-done((f32[1280,2560]{1,0:T(8,128)S(1)}, f32[1280,2560]{1,0:T(8,128)}, u32[]{:S(2)}) %copy-start.1) | copy-done | bytes 13107224
  95.8 4.7 %copy-done.3 = f32[1280,2560]{1,0:T(8,128)S(1)} copy-done((f32[1280,2560]{1,0:T(8,128)S(1)}, f32[1280,2560]{1,0:T(8,128)}, u32[]{:S(2)}) %copy-start.3) | copy-done | bytes 13107224
  100.6 5.9 %apply_down.3 = f32[16,1280]{1,0:T(8,128)S(1)} custom-call(f32[16,5120]{1,0:T(8,128)S(1)} %maximum_divide_fusion.refs_0_, f32[1280,2560]{1,0:T(8,128)S(1)} %copy-done.1, f32[1280,2560]{1,0:T(8,128)S(1)} %copy-done.3, f32[1280,2560]{1,0:T(8,128)} %copy-done.5, f32[1280,2560]{1,0:T(8,128)} %copy-done.7), custom_call_target="tpu_custom_call" | custom-call | tf_op jit(solution)/shard_map/apply_down/pallas_call | solution.py:192
  106.8 5.9 %apply_down.2 = f32[16,1280]{1,0:T(8,128)S(1)} custom-call(f32[16,5120]{1,0:T(8,128)S(1)} %maximum_divide_fusion.refs_0_, f32[1280,2560]{1,0:T(8,128)S(1)} %copy-done.1, f32[1280,2560]{1,0:T(8,128)S(1)} %copy-done.3, f32[1280,2560]{1,0:T(8,128)} %copy-done.5, f32[1280,2560]{1,0:T(8,128)} %copy-done.7), custom_call_target="tpu_custom_call" | custom-call | tf_op jit(solution)/shard_map/apply_down/pallas_call | solution.py:192
  116.9 5.4 %collective-permute-done.19 = f32[24,1280]{1,0:T(8,128)S(1)} collective-permute-done((f32[24,1280]{1,0:T(8,128)S(1)}, f32[24,1280]{1,0:T(8,128)S(1)}, u32[]{:S(2)}, u32[]{:S(2)}) %collective-permute-start.19) | collective-permute-done | bytes 122912 | tf_op jit(solution)/shard_map/ppermute | solution.py:254
  124.9 4.7 %copy-done.8 = f32[1280,2560]{1,0:T(8,128)S(1)} copy-done((f32[1280,2560]{1,0:T(8,128)S(1)}, f32[1280,2560]{1,0:T(8,128)}, u32[]{:S(2)}) %copy-start.8) | copy-done | bytes 13107224
  129.6 9.4 %apply_across.7 = f32[16,1280]{1,0:T(8,128)S(1)} custom-call(f32[16,2560]{1,0:T(8,128)S(1)} %pad_maximum_fusion.1.s_ref, f32[1280,2560]{1,0:T(8,128)S(1)} %copy-done.8), custom_call_target="tpu_custom_call" | custom-call | tf_op jit(solution)/shard_map/apply_across/pallas_call | solution.py:240
  139.1 4.7 %copy-done.6 = f32[1280,2560]{1,0:T(8,128)S(1)} copy-done((f32[1280,2560]{1,0:T(8,128)S(1)}, f32[1280,2560]{1,0:T(8,128)}, u32[]{:S(2)}) %copy-start.6) | copy-done | bytes 13107224
  143.8 9.7 %apply_across.6 = f32[16,1280]{1,0:T(8,128)S(1)} custom-call(f32[16,2560]{1,0:T(8,128)S(1)} %pad_maximum_fusion.1.s_ref, f32[1280,2560]{1,0:T(8,128)S(1)} %copy-done.6), custom_call_target="tpu_custom_call" | custom-call | tf_op jit(solution)/shard_map/apply_across/pallas_call | solution.py:240
  153.5 4.7 %copy-done.4 = f32[1280,2560]{1,0:T(8,128)S(1)} copy-done((f32[1280,2560]{1,0:T(8,128)S(1)}, f32[1280,2560]{1,0:T(8,128)}, u32[]{:S(2)}) %copy-start.4) | copy-done | bytes 13107224
  158.2 3.8 %apply_across.5 = f32[16,1280]{1,0:T(8,128)S(1)} custom-call(f32[16,2560]{1,0:T(8,128)S(1)} %pad_maximum_fusion.1.s_ref, f32[1280,2560]{1,0:T(8,128)S(1)} %copy-done.4), custom_call_target="tpu_custom_call" | custom-call | tf_op jit(solution)/shard_map/apply_across/pallas_call | solution.py:240
  166.2 3.8 %apply_across.4 = f32[16,1280]{1,0:T(8,128)S(1)} custom-call(f32[16,2560]{1,0:T(8,128)S(1)} %pad_maximum_fusion.1.s_ref, f32[1280,2560]{1,0:T(8,128)S(1)} %bitcast.17), custom_call_target="tpu_custom_call" | custom-call | tf_op jit(solution)/shard_map/apply_across/pallas_call | solution.py:240
  170.1 2.4 %collective-permute-start.26 = (f32[16,320]{1,0:T(8,128)S(1)}, f32[16,320]{1,0:T(8,128)S(1)}, u32[]{:S(2)}, u32[]{:S(2)}) collective-permute-start(f32[16,320]{1,0:T(8,128)S(1)} %get-tuple-element.35), channel_id=1, source_target_pairs={{0,6},{2,4},{4,2},{6,0},{1,7},{3,5},{5,3},{7,1},{8,14},{10,12},{12... | collective-permute-start | bytes 61448 | tf_op jit(solution)/shard_map/ppermute | solution.py:254
  175.3 2.6 %collective-permute-done.25 = f32[16,320]{1,0:T(8,128)S(1)} collective-permute-done((f32[16,320]{1,0:T(8,128)S(1)}, f32[16,320]{1,0:T(8,128)S(1)}, u32[]{:S(2)}, u32[]{:S(2)}) %collective-permute-start.25) | collective-permute-done | bytes 20512 | tf_op jit(solution)/shard_map/ppermute | solution.py:254
  (100 shorter events, 29.7 us)
Async XLA Ops:
  2.3 8.4 %collective-permute-start.2 = (f32[80,320]{1,0:T(8,128)S(1)}, f32[80,320]{1,0:T(8,128)S(1)}, u32[]{:S(2)}, u32[]{:S(2)}) collective-permute-start(f32[80,320]{1,0:T(8,128)S(1)} %get-tuple-element.32), channel_id=1, source_target_pairs={{0,96},{32,64},{64,32},{96,0},{1,97},{33,65},{65,33},{97,1},{2,98}... | collective-permute-start | bytes 307208 | tf_op jit(solution)/shard_map/ppermute | solution.py:254
  5.5 7.6 %collective-permute-start.1 = (f32[80,320]{1,0:T(8,128)S(1)}, f32[80,320]{1,0:T(8,128)S(1)}, u32[]{:S(2)}, u32[]{:S(2)}) collective-permute-start(f32[80,320]{1,0:T(8,128)S(1)} %get-tuple-element.32), channel_id=1, source_target_pairs={{0,64},{32,96},{64,0},{96,32},{1,65},{33,97},{65,1},{97,33},{2,66}... | collective-permute-start | bytes 307208 | tf_op jit(solution)/shard_map/ppermute | solution.py:254
  6.1 7.0 %collective-permute-start = (f32[80,320]{1,0:T(8,128)S(1)}, f32[80,320]{1,0:T(8,128)S(1)}, u32[]{:S(2)}, u32[]{:S(2)}) collective-permute-start(f32[80,320]{1,0:T(8,128)S(1)} %get-tuple-element.32), channel_id=1, source_target_pairs={{0,32},{32,0},{64,96},{96,64},{1,33},{33,1},{65,97},{97,65},{2,34}... | collective-permute-start | bytes 307208 | tf_op jit(solution)/shard_map/ppermute | solution.py:254
  13.3 16.6 %collective-permute-start.9 = (f32[64,1280]{1,0:T(8,128)S(1)}, f32[64,1280]{1,0:T(8,128)S(1)}, u32[]{:S(2)}, u32[]{:S(2)}) collective-permute-start(f32[64,1280]{1,0:T(8,128)S(1)} %slice.229), channel_id=1, source_target_pairs={{0,1},{1,0},{2,3},{3,2},{4,5},{5,4},{6,7},{7,6},{8,9},{9,8},{10,11... | collective-permute-start | bytes 983048 | tf_op jit(solution)/shard_map/ppermute | solution.py:254
  13.4 9.9 %collective-permute-start.5 = (f32[80,320]{1,0:T(8,128)S(1)}, f32[80,320]{1,0:T(8,128)S(1)}, u32[]{:S(2)}, u32[]{:S(2)}) collective-permute-start(f32[80,320]{1,0:T(8,128)S(1)} %get-tuple-element.33), channel_id=1, source_target_pairs={{0,6},{2,4},{4,2},{6,0},{1,7},{3,5},{5,3},{7,1},{8,14},{10,12},{12... | collective-permute-start | bytes 307208 | tf_op jit(solution)/shard_map/ppermute | solution.py:254
  17.5 7.7 %collective-permute-start.4 = (f32[80,320]{1,0:T(8,128)S(1)}, f32[80,320]{1,0:T(8,128)S(1)}, u32[]{:S(2)}, u32[]{:S(2)}) collective-permute-start(f32[80,320]{1,0:T(8,128)S(1)} %get-tuple-element.33), channel_id=1, source_target_pairs={{0,4},{2,6},{4,0},{6,2},{1,5},{3,7},{5,1},{7,3},{8,12},{10,14},{12... | collective-permute-start | bytes 307208 | tf_op jit(solution)/shard_map/ppermute | solution.py:254
  17.5 7.7 %collective-permute-start.3 = (f32[80,320]{1,0:T(8,128)S(1)}, f32[80,320]{1,0:T(8,128)S(1)}, u32[]{:S(2)}, u32[]{:S(2)}) collective-permute-start(f32[80,320]{1,0:T(8,128)S(1)} %get-tuple-element.33), channel_id=1, source_target_pairs={{0,2},{2,0},{4,6},{6,4},{1,3},{3,1},{5,7},{7,5},{8,10},{10,8},{12,... | collective-permute-start | bytes 307208 | tf_op jit(solution)/shard_map/ppermute | solution.py:254
  25.3 14.7 %collective-permute-start.6 = (f32[80,1280]{1,0:T(8,128)S(1)}, f32[80,1280]{1,0:T(8,128)S(1)}, u32[]{:S(2)}, u32[]{:S(2)}) collective-permute-start(f32[80,1280]{1,0:T(8,128)S(1)} %concatenate.42.rows_ref), channel_id=1, source_target_pairs={{0,8},{8,0},{16,24},{24,16},{1,9},{9,1},{17,25},{25,17},{2,10},{10... | collective-permute-start | bytes 1228808 | tf_op jit(solution)/shard_map/ppermute | solution.py:254
  28.4 21.8 %collective-permute-start.7 = (f32[80,1280]{1,0:T(8,128)S(1)}, f32[80,1280]{1,0:T(8,128)S(1)}, u32[]{:S(2)}, u32[]{:S(2)}) collective-permute-start(f32[80,1280]{1,0:T(8,128)S(1)} %concatenate.42.rows_ref), channel_id=1, source_target_pairs={{0,16},{8,24},{16,0},{24,8},{1,17},{9,25},{17,1},{25,9},{2,18},{10... | collective-permute-start | bytes 1228808 | tf_op jit(solution)/shard_map/ppermute | solution.py:254
  29.0 33.5 %collective-permute-start.8 = (f32[80,1280]{1,0:T(8,128)S(1)}, f32[80,1280]{1,0:T(8,128)S(1)}, u32[]{:S(2)}, u32[]{:S(2)}) collective-permute-start(f32[80,1280]{1,0:T(8,128)S(1)} %concatenate.42.rows_ref), channel_id=1, source_target_pairs={{0,24},{8,16},{16,8},{24,0},{1,25},{9,17},{17,9},{25,1},{2,26},{10... | collective-permute-start | bytes 1228808 | tf_op jit(solution)/shard_map/ppermute | solution.py:254
  74.4 5.4 %collective-permute-start.11 = (f32[4,4,320]{2,1,0:T(4,128)S(1)}, f32[4,4,320]{2,1,0:T(4,128)S(1)}, u32[]{:S(2)}, u32[]{:S(2)}) collective-permute-start(f32[4,4,320]{2,1,0:T(4,128)S(1)} %pad_maximum_fusion.4), channel_id=1, source_target_pairs={{0,4},{2,6},{4,0},{6,2},{1,5},{3,7},{5,1},{7,3},{8,12},{10,14},{12... | collective-permute-start | bytes 61448 | tf_op jit(solution)/shard_map/ppermute | solution.py:254
  76.7 5.0 %collective-permute-start.12 = (f32[4,4,320]{2,1,0:T(4,128)S(1)}, f32[4,4,320]{2,1,0:T(4,128)S(1)}, u32[]{:S(2)}, u32[]{:S(2)}) collective-permute-start(f32[4,4,320]{2,1,0:T(4,128)S(1)} %pad_maximum_fusion.4), channel_id=1, source_target_pairs={{0,6},{2,4},{4,2},{6,0},{1,7},{3,5},{5,3},{7,1},{8,14},{10,12},{12... | collective-permute-start | bytes 61448 | tf_op jit(solution)/shard_map/ppermute | solution.py:254
  77.8 4.0 %collective-permute-start.10 = (f32[4,4,320]{2,1,0:T(4,128)S(1)}, f32[4,4,320]{2,1,0:T(4,128)S(1)}, u32[]{:S(2)}, u32[]{:S(2)}) collective-permute-start(f32[4,4,320]{2,1,0:T(4,128)S(1)} %pad_maximum_fusion.4), channel_id=1, source_target_pairs={{0,2},{2,0},{4,6},{6,4},{1,3},{3,1},{5,7},{7,5},{8,10},{10,8},{12,... | collective-permute-start | bytes 61448 | tf_op jit(solution)/shard_map/ppermute | solution.py:254
  81.9 4.4 %collective-permute-start.14 = (f32[4,4,320]{2,1,0:T(4,128)S(1)}, f32[4,4,320]{2,1,0:T(4,128)S(1)}, u32[]{:S(2)}, u32[]{:S(2)}) collective-permute-start(f32[4,4,320]{2,1,0:T(4,128)S(1)} %fusion.6), channel_id=1, source_target_pairs={{0,16},{8,24},{16,0},{24,8},{1,17},{9,25},{17,1},{25,9},{2,18},{10... | collective-permute-start | bytes 61448 | tf_op jit(solution)/shard_map/ppermute | solution.py:254
  83.5 5.1 %collective-permute-start.15 = (f32[4,4,320]{2,1,0:T(4,128)S(1)}, f32[4,4,320]{2,1,0:T(4,128)S(1)}, u32[]{:S(2)}, u32[]{:S(2)}) collective-permute-start(f32[4,4,320]{2,1,0:T(4,128)S(1)} %fusion.6), channel_id=1, source_target_pairs={{0,24},{8,16},{16,8},{24,0},{1,25},{9,17},{17,9},{25,1},{2,26},{10... | collective-permute-start | bytes 61448 | tf_op jit(solution)/shard_map/ppermute | solution.py:254
  85.6 5.3 %collective-permute-start.13 = (f32[4,4,320]{2,1,0:T(4,128)S(1)}, f32[4,4,320]{2,1,0:T(4,128)S(1)}, u32[]{:S(2)}, u32[]{:S(2)}) collective-permute-start(f32[4,4,320]{2,1,0:T(4,128)S(1)} %fusion.6), channel_id=1, source_target_pairs={{0,8},{8,0},{16,24},{24,16},{1,9},{9,1},{17,25},{25,17},{2,10},{10... | collective-permute-start | bytes 61448 | tf_op jit(solution)/shard_map/ppermute | solution.py:254
  106.5 6.2 %collective-permute-start.16 = (f32[16,1280]{1,0:T(8,128)S(1)}, f32[16,1280]{1,0:T(8,128)S(1)}, u32[]{:S(2)}, u32[]{:S(2)}) collective-permute-start(f32[16,1280]{1,0:T(8,128)S(1)} %apply_down.3), channel_id=1, source_target_pairs={{0,1},{1,0},{2,3},{3,2},{4,5},{5,4},{6,7},{7,6},{8,9},{9,8},{10,11... | collective-permute-start | bytes 245768 | tf_op jit(solution)/shard_map/ppermute | solution.py:254
  112.7 9.6 %collective-permute-start.19 = (f32[24,1280]{1,0:T(8,128)S(1)}, f32[24,1280]{1,0:T(8,128)S(1)}, u32[]{:S(2)}, u32[]{:S(2)}) collective-permute-start(f32[24,1280]{1,0:T(8,128)S(1)} %select_maximum_fusion), channel_id=1, source_target_pairs={{0,96},{32,64},{64,32},{96,0},{1,97},{33,65},{65,33},{97,1},{2,98}... | collective-permute-start | bytes 368648 | tf_op jit(solution)/shard_map/ppermute | solution.py:254
  114.7 7.7 %collective-permute-start.18 = (f32[24,1280]{1,0:T(8,128)S(1)}, f32[24,1280]{1,0:T(8,128)S(1)}, u32[]{:S(2)}, u32[]{:S(2)}) collective-permute-start(f32[24,1280]{1,0:T(8,128)S(1)} %select_maximum_fusion), channel_id=1, source_target_pairs={{0,64},{32,96},{64,0},{96,32},{1,65},{33,97},{65,1},{97,33},{2,66}... | collective-permute-start | bytes 368648 | tf_op jit(solution)/shard_map/ppermute | solution.py:254
  115.4 7.6 %collective-permute-start.17 = (f32[24,1280]{1,0:T(8,128)S(1)}, f32[24,1280]{1,0:T(8,128)S(1)}, u32[]{:S(2)}, u32[]{:S(2)}) collective-permute-start(f32[24,1280]{1,0:T(8,128)S(1)} %select_maximum_fusion), channel_id=1, source_target_pairs={{0,32},{32,0},{64,96},{96,64},{1,33},{33,1},{65,97},{97,65},{2,34}... | collective-permute-start | bytes 368648 | tf_op jit(solution)/shard_map/ppermute | solution.py:254
  123.5 1.4 collective-permute-start.20
  129.6 36.5 %slice-start = ((s8[13107200]{0:T(1024)(128)(4,1)}), s8[4194304]{0:T(1024)(128)(4,1)S(1)}, s32[]{:S(2)}) async-start(s8[13107200]{0:T(1024)(128)(4,1)} %bitcast.16), calls=%async_computation | async-start | bytes 8388608
  129.6 36.5 %slice-start.1 = ((s8[13107200]{0:T(1024)(128)(4,1)}), s8[4194304]{0:T(1024)(128)(4,1)S(1)}, s32[]{:S(2)}) async-start(s8[13107200]{0:T(1024)(128)(4,1)} %bitcast.16), calls=%async_computation.1 | async-start | bytes 8388608
  143.8 22.4 %slice-start.2 = ((s8[13107200]{0:T(1024)(128)(4,1)}), s8[4194304]{0:T(1024)(128)(4,1)S(1)}, s32[]{:S(2)}) async-start(s8[13107200]{0:T(1024)(128)(4,1)} %bitcast.16), calls=%async_computation.2 | async-start | bytes 8388608
  158.2 8.0 %slice-start.3 = ((s8[13107200]{0:T(1024)(128)(4,1)}), s8[524288]{0:T(1024)(128)(4,1)S(1)}, s32[]{:S(2)}) async-start(s8[13107200]{0:T(1024)(128)(4,1)} %bitcast.16), calls=%async_computation.3 | async-start | bytes 1048576
  158.2 19.7 %copy-start.9 = (f32[320,16]{0,1:T(8,128)S(1)}, f32[320,16]{0,1:T(8,128)}, u32[]{:S(2)}) copy-start(f32[320,16]{0,1:T(8,128)} %param.4) | copy-start | bytes 61444
  162.0 8.0 %collective-permute-start.21 = (f32[16,1280]{1,0:T(8,128)S(1)}, f32[16,1280]{1,0:T(8,128)S(1)}, u32[]{:S(2)}, u32[]{:S(2)}) collective-permute-start(f32[16,1280]{1,0:T(8,128)S(1)} %apply_across.5), channel_id=1, source_target_pairs={{0,8},{8,0},{16,24},{24,16},{1,9},{9,1},{17,25},{25,17},{2,10},{10... | collective-permute-start | bytes 245768 | tf_op jit(solution)/shard_map/ppermute | solution.py:254
  162.8 7.2 %collective-permute-start.22 = (f32[16,1280]{1,0:T(8,128)S(1)}, f32[16,1280]{1,0:T(8,128)S(1)}, u32[]{:S(2)}, u32[]{:S(2)}) collective-permute-start(f32[16,1280]{1,0:T(8,128)S(1)} %apply_across.6), channel_id=1, source_target_pairs={{0,16},{8,24},{16,0},{24,8},{1,17},{9,25},{17,1},{25,9},{2,18},{10... | collective-permute-start | bytes 245768 | tf_op jit(solution)/shard_map/ppermute | solution.py:254
  164.1 5.9 %collective-permute-start.23 = (f32[16,1280]{1,0:T(8,128)S(1)}, f32[16,1280]{1,0:T(8,128)S(1)}, u32[]{:S(2)}, u32[]{:S(2)}) collective-permute-start(f32[16,1280]{1,0:T(8,128)S(1)} %apply_across.7), channel_id=1, source_target_pairs={{0,24},{8,16},{16,8},{24,0},{1,25},{9,17},{17,9},{25,1},{2,26},{10... | collective-permute-start | bytes 245768 | tf_op jit(solution)/shard_map/ppermute | solution.py:254
  170.1 4.1 %collective-permute-start.24 = (f32[16,320]{1,0:T(8,128)S(1)}, f32[16,320]{1,0:T(8,128)S(1)}, u32[]{:S(2)}, u32[]{:S(2)}) collective-permute-start(f32[16,320]{1,0:T(8,128)S(1)} %get-tuple-element.34), channel_id=1, source_target_pairs={{0,2},{2,0},{4,6},{6,4},{1,3},{3,1},{5,7},{7,5},{8,10},{10,8},{12,... | collective-permute-start | bytes 61448 | tf_op jit(solution)/shard_map/ppermute | solution.py:254
  170.1 5.1 %collective-permute-start.26 = (f32[16,320]{1,0:T(8,128)S(1)}, f32[16,320]{1,0:T(8,128)S(1)}, u32[]{:S(2)}, u32[]{:S(2)}) collective-permute-start(f32[16,320]{1,0:T(8,128)S(1)} %get-tuple-element.35), channel_id=1, source_target_pairs={{0,6},{2,4},{4,2},{6,0},{1,7},{3,5},{5,3},{7,1},{8,14},{10,12},{12... | collective-permute-start | bytes 61448 | tf_op jit(solution)/shard_map/ppermute | solution.py:254
  172.5 5.3 %collective-permute-start.25 = (f32[16,320]{1,0:T(8,128)S(1)}, f32[16,320]{1,0:T(8,128)S(1)}, u32[]{:S(2)}, u32[]{:S(2)}) collective-permute-start(f32[16,320]{1,0:T(8,128)S(1)} %get-tuple-element.36), channel_id=1, source_target_pairs={{0,4},{2,6},{4,0},{6,2},{1,5},{3,7},{5,1},{7,3},{8,12},{10,14},{12... | collective-permute-start | bytes 61448 | tf_op jit(solution)/shard_map/ppermute | solution.py:254
  (9 other events, 42.6 us)
